TPU v7x, 32 devices: a whole 2x2x4 slice. The times are simulated.
32 devices in a mesh: parts: 2 (over y), leaf: 4 (over z), col: 2 (over x), rep: 2 (over core).
Axes of the slice: x: 2, y: 2, z: 4, core: 2. Of those that a mesh axis runs over, the one named last changes fastest.
Arguments:
- leaf_inverse: bfloat16 [8, 2048, 2048], P(('parts', 'leaf')), parts along dimension 0, may hold values from -0.125 to 0.125
- leaf_coupling: bfloat16 [8, 2, 128, 2048], P(('parts', 'leaf')), parts along dimension 0, may hold values from -0.0625 to 0.0625
- leaf_rows: int32 [8, 2, 128], P(('parts', 'leaf')), parts along dimension 0, may hold values from 0 to 255, as said below
- leaf_size: int32 [8], P(('parts', 'leaf')), parts along dimension 0, may hold values from 1024 to 2048, as said below
- sep_inverse: bfloat16 [8, 256, 256], P(('parts', 'leaf')), parts along dimension 0, may hold values from -0.375 to 0.375
- sep_coupling: bfloat16 [8, 1, 256, 256], P(('parts', 'leaf')), parts along dimension 0, may hold values from -0.1875 to 0.1875
- rhs_leaf: bfloat16 [16384, 512], P(('parts', 'leaf'), 'col'), parts along dimension 0, may hold values from -6 to 6
- rhs_sep: bfloat16 [2048, 512], P(('parts', 'leaf'), 'col'), parts along dimension 0, may hold values from -6 to 6
- sensor_owner: int32 [4096, 1], P(('parts', 'leaf', 'rep')), parts along dimension 0, may hold values from 0 to 3; in each aligned block of 256 rows (0 to 255, 256 to 511, ...) at most 128 rows name the same one
- sensor_row: int32 [4096], P(('parts', 'leaf', 'rep')), parts along dimension 0, may hold values from 0 to 1023
- sensor_weight: float32 [4096], P(('parts', 'leaf', 'rep')), parts along dimension 0, may hold values from 0.1 to 10
Outputs:
- x_leaf: bfloat16 [16384, 512], P(('parts', 'leaf'), 'col'), parts along dimension 0
- x_sep: bfloat16 [2048, 512], P(('parts', 'leaf'), 'col'), parts along dimension 0
- gram: float32 [1024, 512], P(('parts', 'leaf', 'rep'), 'col'), parts along dimension 0
There are 2 independent parts, one for each index of `parts`. A program takes and returns all parts, laid end to end along the dimension named above; each array names one. Nothing has to cross between parts.
Inputs may be any that keep to these rules, and one draw needn't show every extreme that they name: `leaf_rows`: the 128 row indices of one leaf and level are distinct. `leaf_size`: at least one leaf supernode is full. `sensor_owner`: among the sensors of one device, at most 128 lie in one leaf.
All inputs are finite; a program needn't handle non-finite values.
Results may differ from a plain program's by a relative error of at most 0.0059.
Values may be sent and summed in bfloat16 or wider, within the bound.
A program may use at most 64 MiB of HBM per device.

v0:
```python
import jax
import jax.numpy as jnp
from jax import lax
from jax.sharding import PartitionSpec as P


def from_partner(shard, axis, bit):
    return lax.ppermute(shard, axis, [(i, i ^ 1 << bit) for i in range(lax.axis_size(axis))])


def body(
    leaf_inverse,
    leaf_coupling,
    leaf_rows,
    leaf_size,
    sep_inverse,
    sep_coupling,
    rhs_leaf,
    rhs_sep,
    sensor_owner,
    sensor_row,
    sensor_weight,
):
    groups = lax.axis_size("leaf")
    depth = groups.bit_length() - 1
    place = lax.axis_index("leaf")
    trailing = jnp.zeros((), jnp.int32)
    for bit_count in range(1, depth + 1):
        trailing = trailing + ((place + 1) % 2**bit_count == 0).astype(jnp.int32)
    level = trailing + 1
    ncolumns = rhs_leaf.shape[1]
    leaf_rows_own = leaf_inverse.shape[1]
    sep_rows_own = sep_inverse.shape[1]
    live = (jnp.arange(leaf_rows_own) < leaf_size[0]).astype(jnp.float32)[:, None]
    masked = (rhs_leaf * live).astype(jnp.bfloat16)
    y_leaf = (live * jnp.dot(leaf_inverse[0], masked, preferred_element_type=jnp.float32)).astype(
        jnp.bfloat16
    )
    row_index = leaf_rows[0]
    pending = []
    for height in range(depth):
        product = jnp.dot(leaf_coupling[0, height], y_leaf, preferred_element_type=jnp.float32)
        pending.append(
            jnp.zeros((sep_rows_own, ncolumns), jnp.float32).at[row_index[height]].set(product)
        )
    top_slot = max(depth - 2, 0)
    y_sep = jnp.zeros((sep_rows_own, ncolumns), jnp.bfloat16)
    for height in range(1, depth + 1):
        slot = jnp.clip(height - level - 1, 0, top_slot)
        coupling = lax.dynamic_index_in_dim(sep_coupling[0], slot, 0, keepdims=False)
        partial_sum = pending[height - 1] + jnp.dot(
            coupling, y_sep, preferred_element_type=jnp.float32
        )
        for bit_number in range(height):
            partial_sum = partial_sum + from_partner(partial_sum, "leaf", bit_number)
        g_sep = (rhs_sep.astype(jnp.float32) - partial_sum).astype(jnp.bfloat16)
        solved = jnp.dot(sep_inverse[0], g_sep, preferred_element_type=jnp.float32).astype(
            jnp.bfloat16
        )
        y_sep = jnp.where(level == height, solved, y_sep)
    sep_correction = jnp.zeros((sep_rows_own, ncolumns), jnp.float32)
    leaf_correction = jnp.zeros((leaf_rows_own, ncolumns), jnp.float32)
    x_sep = jnp.zeros((sep_rows_own, ncolumns), jnp.bfloat16)
    for height in range(depth, 0, -1):
        h_sep = (y_sep.astype(jnp.float32) - sep_correction).astype(jnp.bfloat16)
        solved = jnp.dot(sep_inverse[0].T, h_sep, preferred_element_type=jnp.float32).astype(
            jnp.bfloat16
        )
        owner_here = level == height
        x_sep = jnp.where(owner_here, solved, x_sep)
        spread = jnp.where(owner_here, solved, jnp.zeros_like(solved))
        for bit_number in range(height):
            spread = spread + from_partner(spread, "leaf", bit_number)
        slot = jnp.clip(height - level - 1, 0, top_slot)
        coupling = lax.dynamic_index_in_dim(sep_coupling[0], slot, 0, keepdims=False)
        upward = jnp.dot(coupling.T, spread, preferred_element_type=jnp.float32)
        sep_correction = sep_correction + jnp.where(level < height, upward, jnp.zeros_like(upward))
        picked = spread[row_index[height - 1]]
        leaf_correction = leaf_correction + jnp.dot(
            leaf_coupling[0, height - 1].T, picked, preferred_element_type=jnp.float32
        )
    h_leaf = (y_leaf.astype(jnp.float32) - leaf_correction).astype(jnp.bfloat16)
    x_leaf = (live * jnp.dot(leaf_inverse[0].T, h_leaf, preferred_element_type=jnp.float32)).astype(
        jnp.bfloat16
    )
    sensors_here = sensor_owner.shape[0]
    capacity = max(2, 2 * sensors_here // groups)
    owner_ids = sensor_owner[:, 0]
    onehot = (owner_ids[:, None] == jnp.arange(groups, dtype=jnp.int32)[None, :]).astype(jnp.int32)
    within = jnp.sum((jnp.cumsum(onehot, axis=0) - 1) * onehot, axis=1)
    slot_of = owner_ids * capacity + within
    asked_rows = (
        jnp.zeros((groups * capacity,), jnp.int32)
        .at[slot_of]
        .set(sensor_row)
        .reshape(groups, capacity)
    )
    found = x_leaf[lax.all_to_all(asked_rows, "leaf", split_axis=0, concat_axis=0, tiled=True)]
    returned = lax.all_to_all(found, "leaf", split_axis=0, concat_axis=0, tiled=True)
    jacobian = returned.reshape(groups * capacity, ncolumns_full(x_leaf))[slot_of]
    weighted = (sensor_weight[:, None] * jacobian.astype(jnp.float32)).astype(jnp.bfloat16)
    every_column = lax.all_gather(jacobian, "col", axis=1, tiled=True)
    total_sensors = sensors_here * groups * lax.axis_size("rep")
    gram = (
        lax.psum_scatter(
            lax.dot_general(
                every_column, weighted, (((0,), (0,)), ((), ())), preferred_element_type=jnp.float32
            ),
            ("leaf", "rep"),
            scatter_dimension=0,
            tiled=True,
        )
        / total_sensors
    )
    return (x_leaf, x_sep, gram)


def ncolumns_full(x_leaf):
    return x_leaf.shape[1]


def solution(mesh):
    placed = (
        P(("parts", "leaf"), None, None),
        P(("parts", "leaf"), None, None, None),
        P(("parts", "leaf"), None, None),
        P(("parts", "leaf")),
        P(("parts", "leaf"), None, None),
        P(("parts", "leaf"), None, None, None),
        P(("parts", "leaf"), "col"),
        P(("parts", "leaf"), "col"),
        P(("parts", "leaf", "rep"), None),
        P(("parts", "leaf", "rep")),
        P(("parts", "leaf", "rep")),
    )
    return jax.shard_map(
        body,
        mesh=mesh,
        in_specs=placed,
        out_specs=(
            P(("parts", "leaf"), "col"),
            P(("parts", "leaf"), "col"),
            P(("parts", "leaf", "rep"), "col"),
        ),
        check_vma=False,
    )
```

profile of v0, /device:TPU:0, one launch (start us, length us, event | category | flops | bytes accessed | tf_op | source)
XLA Modules:
  0.0 139.6 jit_solution(5281032904196354530)
XLA Ops:
  7.9 6.5 %fusion.14 = bf16[256,2048]{1,0:T(8,128)(2,1)S(1)} fusion(bf16[1,2048,2048]{2,1,0:T(8,128)(2,1)} %param.11, bf16[2048,256]{1,0:T(8,128)(2,1)} %param.17, f32[2048]{0:T(1024)S(1)} %fusion.64), kind=kOutput, calls=%fused_computation.16 | convolution fusion | flops 2150105088 | bytes 10493952 | tf_op jit(solution)/shard_map/dot_general | solution.py:36
  15.1 1.1 scatter_custom_fusion.1
  16.5 3.1 %collective-permute-start = (f32[256,256]{0,1:T(8,128)S(1)}, f32[256,256]{0,1:T(8,128)S(1)}, u32[]{:S(2)}, u32[]{:S(2)}) collective-permute-start(f32[256,256]{0,1:T(8,128)S(1)} %fusion.23), channel_id=1, source_target_pairs={{0,4},{4,0},{8,12},{12,8},{1,5},{5,1},{9,13},{13,9},{2,6},{6,2},{1... | collective-permute-start | bytes 786440 | tf_op jit(solution)/shard_map/ppermute | solution.py:8
  19.7 1.7 %convolution_bitcast_fusion.3 = f32[128,256]{0,1:T(8,128)S(1)} fusion(bf16[256,2048]{1,0:T(8,128)(2,1)} %copy-done.9, bf16[1,2,128,2048]{3,2,1,0:T(8,128)(2,1)S(1)} %copy-done.3), kind=kOutput, calls=%fused_computation.37 | convolution fusion | flops 134217728 | bytes 1703936 | tf_op jit(solution)/shard_map/dot_general | solution.py:42
  21.5 1.1 scatter_custom_fusion
  22.7 3.2 %collective-permute-done = f32[256,256]{0,1:T(8,128)S(1)} collective-permute-done((f32[256,256]{0,1:T(8,128)S(1)}, f32[256,256]{0,1:T(8,128)S(1)}, u32[]{:S(2)}, u32[]{:S(2)}) %collective-permute-start) | collective-permute-done | bytes 262176 | tf_op jit(solution)/shard_map/ppermute | solution.py:8
  26.4 1.8 %collective-permute-start.1 = (f32[256,256]{0,1:T(8,128)S(1)}, f32[256,256]{0,1:T(8,128)S(1)}, u32[]{:S(2)}, u32[]{:S(2)}) collective-permute-start(f32[256,256]{0,1:T(8,128)S(1)} %fusion.22), channel_id=1, source_target_pairs={{0,4},{4,0},{8,12},{12,8},{1,5},{5,1},{9,13},{13,9},{2,6},{6,2},{1... | collective-permute-start | bytes 786440 | tf_op jit(solution)/shard_map/ppermute | solution.py:8
  28.2 1.2 reduce-window.6
  29.7 4.2 %collective-permute-done.1 = f32[256,256]{0,1:T(8,128)S(1)} collective-permute-done((f32[256,256]{0,1:T(8,128)S(1)}, f32[256,256]{0,1:T(8,128)S(1)}, u32[]{:S(2)}, u32[]{:S(2)}) %collective-permute-start.1) | collective-permute-done | bytes 262176 | tf_op jit(solution)/shard_map/ppermute | solution.py:8
  34.0 2.5 %collective-permute-start.2 = (f32[256,256]{0,1:T(8,128)S(1)}, f32[256,256]{0,1:T(8,128)S(1)}, u32[]{:S(2)}, u32[]{:S(2)}) collective-permute-start(f32[256,256]{0,1:T(8,128)S(1)} %add.110), channel_id=1, source_target_pairs={{0,8},{4,12},{8,0},{12,4},{1,9},{5,13},{9,1},{13,5},{2,10},{6,14},... | collective-permute-start | bytes 786440 | tf_op jit(solution)/shard_map/ppermute | solution.py:8
  36.5 10.6 %collective-permute-done.2 = f32[256,256]{0,1:T(8,128)S(1)} collective-permute-done((f32[256,256]{0,1:T(8,128)S(1)}, f32[256,256]{0,1:T(8,128)S(1)}, u32[]{:S(2)}, u32[]{:S(2)}) %collective-permute-start.2) | collective-permute-done | bytes 262176 | tf_op jit(solution)/shard_map/ppermute | solution.py:8
  47.8 2.1 %scatter_custom_fusion.2 = s32[512]{0:T(512)} fusion(s32[256]{0:T(256)S(1)} %bitcast.112, s32[256]{0:T(256)} %param.20, s32[]{:T(128)} %constant.54.clone.1), kind=kCustom, calls=%fused_computation.90 | custom fusion | bytes 2560 | tf_op jit(solution)/shard_map/scatter | solution.py:95
  49.9 4.6 %all-to-all-start = ((s32[4,1,128]{2,1,0:T(1,128)}), s32[4,1,128]{2,1,0:T(1,128)S(1)}, u32[]{:S(2)}, u32[]{:S(2)}) async-start(s32[4,1,128]{2,1,0:T(1,128)} %bitcast.23), calls=%async_computation | async-start | bytes 4096 | tf_op jit(solution)/shard_map/all_to_all | solution.py:98
  54.6 3.0 %collective-permute-start.4 = (bf16[256,256]{0,1:T(8,128)(2,1)S(1)}, bf16[256,256]{0,1:T(8,128)(2,1)S(1)}, u32[]{:S(2)}, u32[]{:S(2)}) collective-permute-start(bf16[256,256]{0,1:T(8,128)(2,1)S(1)} %add.112), channel_id=1, source_target_pairs={{0,8},{4,12},{8,0},{12,4},{1,9},{5,13},{9,1},{13,5},{2,10},{6,14},... | collective-permute-start | bytes 393224 | tf_op jit(solution)/shard_map/ppermute | solution.py:8
  57.6 5.7 %collective-permute-done.4 = bf16[256,256]{0,1:T(8,128)(2,1)S(1)} collective-permute-done((bf16[256,256]{0,1:T(8,128)(2,1)S(1)}, bf16[256,256]{0,1:T(8,128)(2,1)S(1)}, u32[]{:S(2)}, u32[]{:S(2)}) %collective-permute-start.4) | collective-permute-done | bytes 131104 | tf_op jit(solution)/shard_map/ppermute | solution.py:8
  63.3 1.0 broadcast_select_fusion.1
  64.3 0.7 collective-permute-start.5
  65.1 0.8 gather_fusion
  65.9 3.3 %collective-permute-done.5 = bf16[256,256]{0,1:T(8,128)(2,1)S(1)} collective-permute-done((bf16[256,256]{0,1:T(8,128)(2,1)S(1)}, bf16[256,256]{0,1:T(8,128)(2,1)S(1)}, u32[]{:S(2)}, u32[]{:S(2)}) %collective-permute-start.5) | collective-permute-done | bytes 131104 | tf_op jit(solution)/shard_map/ppermute | solution.py:8
  69.4 0.8 gather_fusion.1
  70.2 0.5 fusion.31
  70.7 6.6 %fusion.18 = bf16[2048,256]{0,1:T(8,128)(2,1)S(1)} fusion(bf16[1,2048,2048]{2,1,0:T(8,128)(2,1)} %param.11, f32[256,2048]{1,0:T(8,128)S(1)} %fusion.31, bf16[128,256]{1,0:T(8,128)(2,1)S(1)} %gather_fusion, bf16[256,2048]{1,0:T(8,128)(2,1)} %copy-done.9, f32[2048]{0:T(1024)S(1)} %fusion.64, bf16[1,2,128,2048]{3,2,1,0:T(8,128)(2,1)} %param.12), kind=kOutput, calls=%fused_computation.18 | convolution fusion | flops 2284847104 | bytes 13180928 | tf_op jit(solution)/shard_map/dot_general | solution.py:83
  77.3 0.5 copy.27
  77.9 2.6 %gather_fusion.2 = bf16[512,256]{1,0:T(8,128)(2,1)} fusion(bf16[2048,256]{1,0:T(8,128)(2,1)S(1)} %copy.27, s32[1024]{0:T(1024)S(1)} %pad_clamp_fusion.1), kind=kCustom, calls=%fused_computation.2 | custom fusion | bytes 526336 | tf_op jit(solution)/shard_map/gather | solution.py:98
  80.4 4.9 %all-to-all-start.1 = ((bf16[4,128,256]{2,1,0:T(8,128)(2,1)}), bf16[4,128,256]{2,1,0:T(8,128)(2,1)S(1)}, u32[]{:S(2)}, u32[]{:S(2)}) async-start(bf16[4,128,256]{2,1,0:T(8,128)(2,1)} %bitcast.26), calls=%async_computation.1 | async-start | bytes 524288 | tf_op jit(solution)/shard_map/all_to_all | solution.py:99
  85.4 7.9 %all-to-all-done.1 = bf16[4,128,256]{2,1,0:T(8,128)(2,1)S(1)} async-done(((bf16[4,128,256]{2,1,0:T(8,128)(2,1)}), bf16[4,128,256]{2,1,0:T(8,128)(2,1)S(1)}, u32[]{:S(2)}, u32[]{:S(2)}) %all-to-all-start.1) | async-done | bytes 262176 | tf_op jit(solution)/shard_map/all_to_all | solution.py:99
  93.3 1.2 gather_fusion.3
  94.5 5.6 %all-gather = bf16[256,512]{1,0:T(8,128)(2,1)S(1)} all-gather(bf16[256,256]{1,0:T(8,128)(2,1)S(1)} %gather_fusion.3), channel_id=2, replica_groups=mesh['parts'=2,'leaf'=4,'col'=2,'rep'=2] {'col'}, dimensions={1}, use_global_device_ids=true | all-gather | bytes 393216 | tf_op jit(solution)/shard_map/all_gather | solution.py:102
  100.1 1.1 fusion.45
  101.3 0.8 copy.28
  102.0 29.2 %reduce-scatter.2.cloned.1.call-done = f32[64,256]{1,0:T(8,128)} async-done(((f32[512,256]{1,0:T(8,128)}), f32[64,256]{1,0:T(8,128)}) %reduce-scatter.2.cloned.1.call-update) | async-done | bytes 65552 | tf_op jit(solution)/shard_map/reduce_scatter | solution.py:105
  131.2 1.5 %broadcast_multiply_fusion = f32[64,256]{1,0:T(8,128)} fusion(f32[64,256]{1,0:T(8,128)} %reduce-scatter.2.cloned.1.call-done), kind=kLoop, calls=%fused_computation.72 | loop fusion | flops 16384 | bytes 131072 | tf_op jit(solution)/shard_map/div | solution.py:105
  (58 shorter events, 3.2 us)
Async XLA Ops:
  7.2 18.8 %copy-start = (bf16[1,256,256]{2,1,0:T(8,128)(2,1)S(1)}, bf16[1,256,256]{2,1,0:T(8,128)(2,1)}, u32[]{:S(2)}) copy-start(bf16[1,256,256]{2,1,0:T(8,128)(2,1)} %param.15) | copy-start | bytes 393220
  7.9 6.6 %copy-start.3 = (bf16[1,2,128,2048]{3,2,1,0:T(8,128)(2,1)S(1)}, bf16[1,2,128,2048]{3,2,1,0:T(8,128)(2,1)}, u32[]{:S(2)}) copy-start(bf16[1,2,128,2048]{3,2,1,0:T(8,128)(2,1)} %param.12) | copy-start | bytes 3145732
  7.9 7.1 %copy-start.7 = (s32[1,2,128]{2,1,0:T(2,128)S(1)}, s32[1,2,128]{2,1,0:T(2,128)}, u32[]{:S(2)}) copy-start(s32[1,2,128]{2,1,0:T(2,128)} %param.13) | copy-start | bytes 3076
  14.5 5.2 %copy-start.9 = (bf16[256,2048]{1,0:T(8,128)(2,1)}, bf16[256,2048]{1,0:T(8,128)(2,1)S(1)}, u32[]{:S(2)}) copy-start(bf16[256,2048]{1,0:T(8,128)(2,1)S(1)} %fusion.14) | copy-start | bytes 3145732
  14.5 1.8 %copy-start.2 = (bf16[1,1,256,256]{3,2,1,0:T(8,128)(2,1)S(1)}, bf16[1,1,256,256]{3,2,1,0:T(8,128)(2,1)}, u32[]{:S(2)}) copy-start(bf16[1,1,256,256]{3,2,1,0:T(8,128)(2,1)} %param.16) | copy-start | bytes 393220
  14.5 5.1 %copy-start.4 = (bf16[256,256]{1,0:T(8,128)(2,1)S(1)}, bf16[256,256]{1,0:T(8,128)(2,1)}, u32[]{:S(2)}) copy-start(bf16[256,256]{1,0:T(8,128)(2,1)} %param.18) | copy-start | bytes 393220
  16.5 9.4 %collective-permute-start = (f32[256,256]{0,1:T(8,128)S(1)}, f32[256,256]{0,1:T(8,128)S(1)}, u32[]{:S(2)}, u32[]{:S(2)}) collective-permute-start(f32[256,256]{0,1:T(8,128)S(1)} %fusion.23), channel_id=1, source_target_pairs={{0,4},{4,0},{8,12},{12,8},{1,5},{5,1},{9,13},{13,9},{2,6},{6,2},{1... | collective-permute-start | bytes 786440 | tf_op jit(solution)/shard_map/ppermute | solution.py:8
  19.7 8.5 %copy-start.6 = (s32[256,1]{0,1:T(1,128)S(1)}, s32[256,1]{0,1:T(1,128)}, u32[]{:S(2)}) copy-start(s32[256,1]{0,1:T(1,128)} %param.19) | copy-start | bytes 3076
  26.4 7.6 %collective-permute-start.1 = (f32[256,256]{0,1:T(8,128)S(1)}, f32[256,256]{0,1:T(8,128)S(1)}, u32[]{:S(2)}, u32[]{:S(2)}) collective-permute-start(f32[256,256]{0,1:T(8,128)S(1)} %fusion.22), channel_id=1, source_target_pairs={{0,4},{4,0},{8,12},{12,8},{1,5},{5,1},{9,13},{13,9},{2,6},{6,2},{1... | collective-permute-start | bytes 786440 | tf_op jit(solution)/shard_map/ppermute | solution.py:8
  34.0 13.1 %collective-permute-start.2 = (f32[256,256]{0,1:T(8,128)S(1)}, f32[256,256]{0,1:T(8,128)S(1)}, u32[]{:S(2)}, u32[]{:S(2)}) collective-permute-start(f32[256,256]{0,1:T(8,128)S(1)} %add.110), channel_id=1, source_target_pairs={{0,8},{4,12},{8,0},{12,4},{1,9},{5,13},{9,1},{13,5},{2,10},{6,14},... | collective-permute-start | bytes 786440 | tf_op jit(solution)/shard_map/ppermute | solution.py:8
  47.5 7.0 %collective-permute-start.3 = (bf16[256,256]{0,1:T(8,128)(2,1)S(1)}, bf16[256,256]{0,1:T(8,128)(2,1)S(1)}, u32[]{:S(2)}, u32[]{:S(2)}) collective-permute-start(bf16[256,256]{0,1:T(8,128)(2,1)S(1)} %fusion.29), channel_id=1, source_target_pairs={{0,4},{4,0},{8,12},{12,8},{1,5},{5,1},{9,13},{13,9},{2,6},{6,2},{1... | collective-permute-start | bytes 393224 | tf_op jit(solution)/shard_map/ppermute | solution.py:8
  49.9 15.0 %all-to-all-start = ((s32[4,1,128]{2,1,0:T(1,128)}), s32[4,1,128]{2,1,0:T(1,128)S(1)}, u32[]{:S(2)}, u32[]{:S(2)}) async-start(s32[4,1,128]{2,1,0:T(1,128)} %bitcast.23), calls=%async_computation | async-start | bytes 4096 | tf_op jit(solution)/shard_map/all_to_all | solution.py:98
  54.6 8.7 %collective-permute-start.4 = (bf16[256,256]{0,1:T(8,128)(2,1)S(1)}, bf16[256,256]{0,1:T(8,128)(2,1)S(1)}, u32[]{:S(2)}, u32[]{:S(2)}) collective-permute-start(bf16[256,256]{0,1:T(8,128)(2,1)S(1)} %add.112), channel_id=1, source_target_pairs={{0,8},{4,12},{8,0},{12,4},{1,9},{5,13},{9,1},{13,5},{2,10},{6,14},... | collective-permute-start | bytes 393224 | tf_op jit(solution)/shard_map/ppermute | solution.py:8
  64.3 5.0 %collective-permute-start.5 = (bf16[256,256]{0,1:T(8,128)(2,1)S(1)}, bf16[256,256]{0,1:T(8,128)(2,1)S(1)}, u32[]{:S(2)}, u32[]{:S(2)}) collective-permute-start(bf16[256,256]{0,1:T(8,128)(2,1)S(1)} %get-tuple-element.7), channel_id=1, source_target_pairs={{0,4},{4,0},{8,12},{12,8},{1,5},{5,1},{9,13},{13,9},{2,6},{6,2},{1... | collective-permute-start | bytes 393224 | tf_op jit(solution)/shard_map/ppermute | solution.py:8
  77.8 22.3 %copy-start.1 = (bf16[2048,256]{1,0:T(8,128)(2,1)}, bf16[2048,256]{1,0:T(8,128)(2,1)S(1)}, u32[]{:S(2)}) copy-start(bf16[2048,256]{1,0:T(8,128)(2,1)S(1)} %copy.27) | copy-start | bytes 3145732
  77.8 22.3 %copy-start.8 = (f32[256]{0:T(256)S(1)}, f32[256]{0:T(256)}, u32[]{:S(2)}) copy-start(f32[256]{0:T(256)} %param.21) | copy-start | bytes 3076
  80.4 20.8 %copy-start.5 = (bf16[256,256]{0,1:T(8,128)(2,1)S(1)}, bf16[256,256]{0,1:T(8,128)(2,1)}, u32[]{:S(2)}) copy-start(bf16[256,256]{0,1:T(8,128)(2,1)} %get-tuple-element.6) | copy-start | bytes 393220
  80.4 12.9 %all-to-all-start.1 = ((bf16[4,128,256]{2,1,0:T(8,128)(2,1)}), bf16[4,128,256]{2,1,0:T(8,128)(2,1)S(1)}, u32[]{:S(2)}, u32[]{:S(2)}) async-start(bf16[4,128,256]{2,1,0:T(8,128)(2,1)} %bitcast.26), calls=%async_computation.1 | async-start | bytes 524288 | tf_op jit(solution)/shard_map/all_to_all | solution.py:99
  85.4 45.9 %reduce-scatter.2.cloned.1.call-start = ((), (), s32[]{:S(2)}) async-start(), calls=%async_computation.3 | async-start | bytes 589824 | tf_op jit(solution)/shard_map/reduce_scatter | solution.py:105
Sparse Core Ops, SparseCore 0:
  101.4 29.8 reduce-scatter.1
where the time goes:
time: 140 us
  waiting for transfers between devices  64.1 us (46%)
  starting transfers between devices  20.9 us (15%)
  matrix products  18.9 us (13%)
  between operations  15 us (11%)
  local copies, waits for them, and re-layouts  12.1 us (9%)
  blocking collectives  5.64 us (4%)
  other arithmetic  3 us (2%)
    reduce_scatter x1, waiting for transfers between devices, body(): lax.psum_scatter(lax.dot_general(every_column, weighted, (((0,), (0,)), (...  29.2 us
    ppermute x6, waiting for transfers between devices, from_partner(): lax.ppermute(shard, axis, [(i, i ^ 1 << bit) for i in range(lax.axis_size...  27 us
    ppermute x6, starting transfers between devices, from_partner(): lax.ppermute(shard, axis, [(i, i ^ 1 << bit) for i in range(lax.axis_size...  11.3 us
    all_to_all x1, waiting for transfers between devices, body(): lax.all_to_all(found, 'leaf', split_axis=0, concat_axis=0, tiled=True)  7.94 us
    dot_general x1, matrix products, body(): jnp.dot(leaf_inverse[0].T, h_leaf, preferred_element_type=jnp.float32)  6.59 us
    dot_general x1, matrix products, body(): jnp.dot(leaf_inverse[0], masked, preferred_element_type=jnp.float32)  6.54 us
    all_gather x1, blocking collectives, body(): every_column = lax.all_gather(jacobian, 'col', axis=1, tiled=True)  5.64 us
    all_to_all x1, starting transfers between devices, body(): lax.all_to_all(found, 'leaf', split_axis=0, concat_axis=0, tiled=True)  4.92 us
  transfers between devices with their start and end apart: 9, of which 7 were waited for; matrix products, arithmetic and copies ran while one was open for 7% of the time, Pallas kernels for 0%

commit v1 on v0

v1 whole, which is shorter than its diff:
```python
import functools

import jax
import jax.numpy as jnp
from jax import lax
from jax.experimental import pallas as pl
from jax.experimental.pallas import tpu as pltpu
from jax.sharding import PartitionSpec as P

F32, BF16 = jnp.float32, jnp.bfloat16
NN = (((1,), (0,)), ((), ()))
NT = (((1,), (1,)), ((), ()))
TN = (((0,), (0,)), ((), ()))
CHUNK = 256
LANES = 128


def mm(a, b, dims=NN):
    return lax.dot_general(a, b, dims, preferred_element_type=F32)


def remote(src, dst, send_sem, recv_sem, **place):
    return pltpu.make_async_remote_copy(
        src_ref=src,
        dst_ref=dst,
        send_sem=send_sem,
        recv_sem=recv_sem,
        device_id=place,
        device_id_type=pl.DeviceIdType.MESH,
    )


def kernel(
    n,
    reps,
    cols,
    total_sensors,
    a_hbm,
    coup_hbm,
    rows_ref,
    size_ref,
    s_hbm,
    u_hbm,
    b_hbm,
    rhs_hbm,
    owner_ref,
    srow_ref,
    weight_ref,
    xleaf_hbm,
    xsep_ref,
    gram_ref,
    a_v,
    b_v,
    coup_v,
    spread_v,
    y_v,
    h_v,
    x_v,
    xo_v,
    wx_v,
    s_anc,
    u_anc,
    r_anc,
    part_v,
    sbuf,
    rbuf,
    ysep,
    xfull,
    tab,
    tab_in,
    wpad,
    wcol,
    gs,
    gin,
    a_sem,
    in_sem,
    out_sem,
    anc_send,
    anc_recv,
    tab_send,
    tab_recv,
    bf_send,
    bf_recv,
    xs_send,
    xs_recv,
    col_send,
    col_recv,
    gr_send,
    gr_recv,
):
    depth = n.bit_length() - 1
    ls, nc = b_v.shape
    ss = s_anc.shape[1]
    hc = r_anc.shape[2]
    split = hc < nc
    sens_rows = xo_v.shape[1]
    nhi = sens_rows // LANES
    rb = gin.shape[1]
    per = hc // rb
    i = lax.axis_index("leaf")
    c = lax.axis_index("col")
    r = lax.axis_index("rep")
    half = pl.ds(pl.multiple_of(r * hc, hc), hc) if split else pl.ds(0, nc)
    nchunk = ls // CHUNK

    load_b = pltpu.make_async_copy(b_hbm, b_v, in_sem.at[0])
    load_b.start()
    load_c = pltpu.make_async_copy(coup_hbm.at[0], coup_v, in_sem.at[1])
    load_c.start()
    loads = [
        pltpu.make_async_copy(
            a_hbm.at[0, pl.ds(k * CHUNK, CHUNK)], a_v.at[pl.ds(k * CHUNK, CHUNK)], a_sem.at[k]
        )
        for k in range(nchunk)
    ]
    for load in loads:
        load.start()

    barrier = pltpu.get_barrier_semaphore()

    def greet(**place):
        pl.semaphore_signal(barrier, inc=1, device_id=place, device_id_type=pl.DeviceIdType.MESH)

    for j in range(n):
        for q in range(reps):
            @pl.when(jnp.logical_not((i == j) & (r == q)))
            def _():
                greet(leaf=j, rep=q)
    for step in range(1, cols):
        greet(col=lax.rem(c + step, cols))
    pl.semaphore_wait(barrier, n * reps + cols - 2)

    def anc_copies(level, slot):
        base = i // 2**level * 2**level
        dest = base + slot
        copies = [
            (s_hbm.at[0], s_anc.at[level - 1], 0),
            (rhs_hbm.at[:, half], r_anc.at[level - 1], 1),
        ]
        if level < depth:
            copies.append((u_hbm.at[0], u_anc.at[level - 1], 2))
        return dest, copies

    def owner_of(level):
        return i // 2**level * 2**level + 2 ** (level - 1) - 1

    for level in range(1, depth + 1):
        for slot in range(2**level):
            dest, copies = anc_copies(level, slot)

            @pl.when((i == owner_of(level)) & (dest == i))
            def _():
                for src, dst, kind in copies:
                    pltpu.make_async_copy(src, dst, anc_recv.at[level - 1, kind]).start()

            @pl.when((i == owner_of(level)) & (dest != i))
            def _():
                for src, dst, kind in copies:
                    remote(
                        src, dst, anc_send.at[slot, kind], anc_recv.at[level - 1, kind], leaf=dest
                    ).start()

    hi_key = owner_ref[...] * nhi + srow_ref[...] // LANES
    lo_key = srow_ref[...] % LANES
    sensors = hi_key.shape[1]
    hi_hot = (lax.broadcasted_iota(jnp.int32, (n * nhi, sensors), 0) == hi_key).astype(F32)
    hi_hot = hi_hot.astype(BF16)
    lo_hot = lax.broadcasted_iota(jnp.int32, (LANES, sensors), 0) == lo_key
    rest = weight_ref[...]
    table = jnp.zeros((n * nhi, LANES), F32)
    for _ in range(3):
        piece = rest.astype(BF16).astype(F32)
        table = table + mm(hi_hot, jnp.where(lo_hot, piece, 0.0).astype(BF16), NT)
        rest = rest - piece
    tab[...] = table
    here = i * reps + r
    for j in range(n):
        for q in range(reps):
            own = (i == j) & (r == q)

            @pl.when(own)
            def _():
                tab_in[here] = tab[pl.ds(j * nhi, nhi), :]

            @pl.when(jnp.logical_not(own))
            def _():
                remote(
                    tab.at[pl.ds(j * nhi, nhi)],
                    tab_in.at[here],
                    tab_send.at[j * reps + q],
                    tab_recv.at[here],
                    leaf=j,
                    rep=q,
                ).start()

    size = size_ref[0]

    def live(k):
        return lax.broadcasted_iota(jnp.int32, (CHUNK, nc), 0) + k * CHUNK < size

    load_b.wait()
    for k in range(nchunk):
        rows = pl.ds(k * CHUNK, CHUNK)
        b_v[rows, :] = jnp.where(live(k), b_v[rows, :].astype(F32), 0.0).astype(BF16)
    load_c.wait()
    for level in range(depth):
        hot = lax.broadcasted_iota(jnp.int32, (ss, rows_ref.shape[2]), 0) == rows_ref[
            0, pl.ds(level, 1), :
        ]
        spread_v[pl.ds(level * ss, ss), :] = mm(
            hot.astype(F32).astype(BF16), coup_v[level]
        ).astype(BF16)
    for k in range(nchunk):
        rows = pl.ds(k * CHUNK, CHUNK)
        loads[k].wait()
        y_v[rows, :] = jnp.where(live(k), mm(a_v[rows, :], b_v[...]), 0.0).astype(BF16)
        product = mm(spread_v[:, rows], y_v[rows, half])
        part_v[...] = product if k == 0 else part_v[...] + product

    def wait_anc(level, kind):
        _, copies = anc_copies(level, 0)
        src, dst, which = copies[kind]
        pltpu.make_async_copy(src, dst, anc_recv.at[level - 1, which]).wait()

    sent = []
    for level in range(1, depth + 1):
        partner = i ^ (1 << (level - 1))
        stage = level - 1
        pieces = [(pl.ds(level - 1, 1), 0)]
        if level < depth:
            pieces.append((pl.ds(level, depth - level), 1))
        copies = []
        for span, which in pieces:
            for m in range(span.start, span.start + span.size):
                sbuf[stage, m] = part_v[pl.ds(m * ss, ss), :].astype(BF16)
            copy = remote(
                sbuf.at[stage, span],
                rbuf.at[stage, span],
                bf_send.at[stage, which],
                bf_recv.at[stage, which],
                leaf=partner,
            )
            copy.start()
            copies.append(copy)
        sent += copies
        if level == 1:
            for j in range(n):
                for q in range(reps):
                    @pl.when(jnp.logical_not((i == j) & (r == q)))
                    def _():
                        remote(
                            tab.at[pl.ds(0, nhi)],
                            tab_in.at[j * reps + q],
                            tab_send.at[0],
                            tab_recv.at[j * reps + q],
                            rep=1 - r,
                        ).wait_recv()
            wpad[...] = jnp.zeros_like(wpad)
            weights = tab_in[0]
            for j in range(1, n * reps):
                weights = weights + tab_in[j]
            wpad[pl.ds(0, nhi), :] = weights
            wcol[...] = wpad[...].T
        wait_anc(level, 0)
        wait_anc(level, 1)
        if level < depth:
            wait_anc(level, 2)
        copies[0].wait_recv()
        total = part_v[pl.ds(stage * ss, ss), :] + rbuf[stage, stage].astype(F32)
        g = (r_anc[stage].astype(F32) - total).astype(BF16)
        y_here = mm(s_anc[stage], g).astype(BF16)
        ysep[stage] = y_here
        if level < depth:
            copies[1].wait_recv()
            for m in range(level, depth):
                span = pl.ds(m * ss, ss)
                part_v[span, :] = (
                    part_v[span, :]
                    + rbuf[stage, m].astype(F32)
                    + mm(u_anc[stage, m - level], y_here)
                )

    solved = {}
    shared = []
    for level in range(depth, 0, -1):
        stage = level - 1
        h_here = ysep[stage]
        if level < depth:
            correction = mm(u_anc[stage, 0], solved[level + 1], TN)
            for upper in range(level + 2, depth + 1):
                correction = correction + mm(u_anc[stage, upper - level - 1], solved[upper], TN)
            h_here = (h_here.astype(F32) - correction).astype(BF16)
        solved[level] = mm(s_anc[stage], h_here, TN).astype(BF16)
        span = pl.ds(stage * ss, ss)
        xfull[span, half] = solved[level]
        if split:
            copy = remote(
                xfull.at[span, half], xfull.at[span, half], xs_send.at[stage], xs_recv.at[stage],
                rep=1 - r,
            )
            copy.start()
            shared.append(copy)
    sent += shared
    for copy in shared:
        copy.wait_recv()
    for k in range(nchunk):
        rows = pl.ds(k * CHUNK, CHUNK)
        h_v[rows, :] = (
            y_v[rows, :].astype(F32) - mm(spread_v[:, rows], xfull[...], TN)
        ).astype(BF16)

    outs = []
    from_col = {}

    def back_solve(k):
        rows = pl.ds(k * CHUNK, CHUNK)
        x_v[rows, :] = jnp.where(live(k), mm(a_v[:, rows], h_v[...], TN), 0.0).astype(BF16)
        if k * CHUNK < sens_rows:
            for step in range(1, cols):
                copy = remote(
                    x_v.at[rows, half],
                    xo_v.at[step - 1, rows],
                    col_send.at[step - 1, k],
                    col_recv.at[step - 1, k],
                    col=lax.rem(c + step, cols),
                )
                copy.start()
                from_col[step, k] = copy
        out = pltpu.make_async_copy(x_v.at[rows], xleaf_hbm.at[rows], out_sem.at[k])
        out.start()
        outs.append(out)

    nsens = sens_rows // CHUNK
    for k in range(nsens):
        back_solve(k)
    sent += list(from_col.values())
    for k in range(nhi):
        rows = pl.ds(k * LANES, LANES)
        wx_v[rows, :] = (x_v[rows, :].astype(F32) * wcol[:, k : k + 1]).astype(BF16)

    def scatter_gram(b, wait):
        block = lax.rem(c + cols - b, cols)
        group = block * reps + r if split else block
        for t in range(per):
            dest = group * per + t
            if not split and t % reps == 0:
                dest = dest + r
            elif not split:
                continue
            own = (dest // reps == i) & (dest % reps == r)
            span = pl.ds(t * rb, rb) if split else pl.ds(pl.multiple_of((t + r) * rb, rb), rb)

            if not wait:
                @pl.when(own)
                def _():
                    gin[i] = gs[b, span, :]

            @pl.when(jnp.logical_not(own))
            def _():
                copy = remote(
                    gs.at[b, span],
                    gin.at[i],
                    gr_send.at[b, t],
                    gr_recv.at[i],
                    leaf=dest // reps,
                    rep=dest % reps,
                )
                if wait:
                    copy.wait_send()
                else:
                    copy.start()

    gs[0] = mm(x_v[pl.ds(0, sens_rows), half], wx_v[...], TN).astype(gs.dtype)
    scatter_gram(0, False)
    for k in range(nsens, nchunk):
        back_solve(k)
    for b in range(1, cols):
        other = jnp.zeros((hc, nc), F32)
        for k in range(nsens):
            rows = pl.ds(k * CHUNK, CHUNK)
            from_col[b, k].wait_recv()
            other = other + mm(xo_v[b - 1, rows, :], wx_v[rows, :], TN)
        gs[b] = other.astype(gs.dtype)
        scatter_gram(b, False)

    xsep_ref[...] = jnp.zeros_like(xsep_ref)
    for level in range(1, depth + 1):
        @pl.when(i == owner_of(level))
        def _():
            xsep_ref[...] = xfull[pl.ds((level - 1) * ss, ss), :]

    for copy in sent:
        copy.wait_send()
    for level in range(1, depth + 1):
        for slot in range(2**level):
            dest, copies = anc_copies(level, slot)

            @pl.when((i == owner_of(level)) & (dest != i))
            def _():
                for src, dst, kind in copies:
                    remote(
                        src, dst, anc_send.at[slot, kind], anc_recv.at[level - 1, kind], leaf=dest
                    ).wait_send()
    for j in range(n):
        for q in range(reps):
            @pl.when(jnp.logical_not((i == j) & (r == q)))
            def _():
                remote(
                    tab.at[pl.ds(j * nhi, nhi)],
                    tab_in.at[here],
                    tab_send.at[j * reps + q],
                    tab_recv.at[here],
                    leaf=j,
                    rep=q,
                ).wait_send()
    for out in outs:
        out.wait()

    sender = here // per % reps if split else r
    for j in range(n):
        @pl.when(jnp.logical_not((i == j) & (sender == r)))
        def _():
            remote(
                gs.at[0, pl.ds(0, rb)], gin.at[j], gr_send.at[0, 0], gr_recv.at[j], rep=1 - r
            ).wait_recv()
    gram = gin[0].astype(F32)
    for j in range(1, n):
        gram = gram + gin[j].astype(F32)
    gram_ref[...] = gram / total_sensors
    for b in range(cols):
        scatter_gram(b, True)


def body(
    leaf_inverse,
    leaf_coupling,
    leaf_rows,
    leaf_size,
    sep_inverse,
    sep_coupling,
    rhs_leaf,
    rhs_sep,
    sensor_owner,
    sensor_row,
    sensor_weight,
):
    n = lax.axis_size("leaf")
    reps = lax.axis_size("rep")
    cols = lax.axis_size("col")
    depth = n.bit_length() - 1
    ls, nc = rhs_leaf.shape
    ss = sep_inverse.shape[1]
    kr = leaf_coupling.shape[2]
    slots = sep_coupling.shape[1]
    hc = nc // reps if nc // reps % LANES == 0 else nc
    sens = sensor_row.shape[0]
    sens_rows = ls // 2
    nhi = sens_rows // LANES
    rb = nc * cols // (n * reps)
    gram_type = BF16 if rb % 16 == 0 else F32
    nchunk = ls // CHUNK
    dma = pltpu.SemaphoreType.DMA
    hbm = pl.BlockSpec(memory_space=pl.ANY)
    vmem = pl.BlockSpec(memory_space=pltpu.VMEM)
    smem = pl.BlockSpec(memory_space=pltpu.SMEM)
    return pl.pallas_call(
        functools.partial(kernel, n, reps, cols, sens * n * reps),
        out_shape=(
            jax.ShapeDtypeStruct((ls, nc), BF16),
            jax.ShapeDtypeStruct((ss, nc), BF16),
            jax.ShapeDtypeStruct((rb, nc), F32),
        ),
        in_specs=[hbm, hbm, vmem, smem, hbm, hbm, hbm, hbm, vmem, vmem, vmem],
        out_specs=(hbm, vmem, vmem),
        scratch_shapes=[
            pltpu.VMEM((ls, ls), BF16),
            pltpu.VMEM((ls, nc), BF16),
            pltpu.VMEM((depth, kr, ls), BF16),
            pltpu.VMEM((depth * ss, ls), BF16),
            pltpu.VMEM((ls, nc), BF16),
            pltpu.VMEM((ls, nc), BF16),
            pltpu.VMEM((ls, nc), BF16),
            pltpu.VMEM((cols - 1, sens_rows, hc), BF16),
            pltpu.VMEM((sens_rows, nc), BF16),
            pltpu.VMEM((depth, ss, ss), BF16),
            pltpu.VMEM((depth, slots, ss, ss), BF16),
            pltpu.VMEM((depth, ss, hc), BF16),
            pltpu.VMEM((depth * ss, hc), F32),
            pltpu.VMEM((depth, depth, ss, hc), BF16),
            pltpu.VMEM((depth, depth, ss, hc), BF16),
            pltpu.VMEM((depth, ss, hc), BF16),
            pltpu.VMEM((depth * ss, nc), BF16),
            pltpu.VMEM((n * nhi, LANES), F32),
            pltpu.VMEM((n * reps, nhi, LANES), F32),
            pltpu.VMEM((LANES, LANES), F32),
            pltpu.VMEM((LANES, LANES), F32),
            pltpu.VMEM((cols, hc, nc), gram_type),
            pltpu.VMEM((n, rb, nc), gram_type),
            dma((nchunk,)),
            dma((2,)),
            dma((nchunk,)),
            dma((n, 3)),
            dma((depth, 3)),
            dma((n * reps,)),
            dma((n * reps,)),
            dma((depth, 2)),
            dma((depth, 2)),
            dma((depth,)),
            dma((depth,)),
            dma((cols - 1, nchunk)),
            dma((cols - 1, nchunk)),
            dma((cols, hc // rb)),
            dma((n,)),
        ],
        compiler_params=pltpu.CompilerParams(
            collective_id=0, has_side_effects=True, vmem_limit_bytes=52 * 2**20
        ),
        name="solve_and_gram",
    )(
        leaf_inverse,
        leaf_coupling,
        leaf_rows,
        leaf_size,
        sep_inverse,
        sep_coupling,
        rhs_leaf,
        rhs_sep,
        sensor_owner.reshape(1, sens),
        sensor_row.reshape(1, sens),
        sensor_weight.reshape(1, sens),
    )


def solution(mesh):
    placed = (
        P(("parts", "leaf"), None, None),
        P(("parts", "leaf"), None, None, None),
        P(("parts", "leaf"), None, None),
        P(("parts", "leaf")),
        P(("parts", "leaf"), None, None),
        P(("parts", "leaf"), None, None, None),
        P(("parts", "leaf"), "col"),
        P(("parts", "leaf"), "col"),
        P(("parts", "leaf", "rep"), None),
        P(("parts", "leaf", "rep")),
        P(("parts", "leaf", "rep")),
    )
    return jax.shard_map(
        body,
        mesh=mesh,
        in_specs=placed,
        out_specs=(
            P(("parts", "leaf"), "col"),
            P(("parts", "leaf"), "col"),
            P(("parts", "leaf", "rep"), "col"),
        ),
        check_vma=False,
    )
```

time: 140 us -> 47.2 us (0.34)
  the two profiles are of different devices: /device:TPU:0 before, /device:TPU:17 now
where the time goes in v1:
time: 47.2 us; the launch traced here: 47 us
  Pallas kernels  38 us (81%)
  local copies, waits for them, and re-layouts  7.67 us (16%)
  between operations  1.3 us (3%)
    pallas_call x1, Pallas kernels, body(): pl.pallas_call(functools.partial(kernel, n, reps, cols, sens * n * reps),...  38 us
    unnamed x17, local copies, waits for them, and re-layouts  7.67 us

profile of v1, /device:TPU:17, one launch (start us, length us, event | category | flops | bytes accessed | tf_op | source)
XLA Modules:
  0.0 47.0 jit_solution(15310193930083658322)
XLA Ops:
  1.3 0.0 copy-start
  1.3 0.9 %copy-done = bf16[1,256,256]{2,1,0:T(8,128)(2,1)S(1)} copy-done((bf16[1,256,256]{2,1,0:T(8,128)(2,1)S(1)}, bf16[1,256,256]{2,1,0:T(8,128)(2,1)}, u32[]{:S(2)}) %copy-start) | copy-done | bytes 131096
  2.2 0.0 copy-start.1
  2.2 0.9 %copy-done.1 = bf16[1,1,256,256]{3,2,1,0:T(8,128)(2,1)S(1)} copy-done((bf16[1,1,256,256]{3,2,1,0:T(8,128)(2,1)S(1)}, bf16[1,1,256,256]{3,2,1,0:T(8,128)(2,1)}, u32[]{:S(2)}) %copy-start.1) | copy-done | bytes 131096
  3.1 0.0 copy-start.2
  3.1 0.9 %copy-done.2 = bf16[256,256]{1,0:T(8,128)(2,1)S(1)} copy-done((bf16[256,256]{1,0:T(8,128)(2,1)S(1)}, bf16[256,256]{1,0:T(8,128)(2,1)}, u32[]{:S(2)}) %copy-start.2) | copy-done | bytes 131096
  4.0 0.0 copy-start.3
  4.0 0.7 %copy-done.3 = s32[1,2,128]{2,1,0:T(2,128)S(1)} copy-done((s32[1,2,128]{2,1,0:T(2,128)S(1)}, s32[1,2,128]{2,1,0:T(2,128)}, u32[]{:S(2)}) %copy-start.3) | copy-done | bytes 1048
  4.7 0.0 copy-start.4
  4.7 0.7 %copy-done.4 = s32[256,1]{0,1:T(1,128)S(1)} copy-done((s32[256,1]{0,1:T(1,128)S(1)}, s32[256,1]{0,1:T(1,128)}, u32[]{:S(2)}) %copy-start.4) | copy-done | bytes 1048
  5.4 0.0 copy-start.5
  5.4 0.7 %copy-done.5 = s32[256]{0:T(256)S(1)} copy-done((s32[256]{0:T(256)S(1)}, s32[256]{0:T(256)}, u32[]{:S(2)}) %copy-start.5) | copy-done | bytes 1048
  6.0 0.0 copy-start.6
  6.0 0.7 %copy-done.6 = f32[256]{0:T(256)S(1)} copy-done((f32[256]{0:T(256)S(1)}, f32[256]{0:T(256)}, u32[]{:S(2)}) %copy-start.6) | copy-done | bytes 1048
  6.7 38.0 %solve_and_gram.1 = (bf16[2048,256]{1,0:T(8,128)(2,1)S(1)}, bf16[256,256]{1,0:T(8,128)(2,1)S(1)}, f32[64,256]{1,0:T(8,128)S(1)}) custom-call(bf16[1,2048,2048]{2,1,0:T(8,128)(2,1)} %a_hbm.1, bf16[1,2,128,2048]{3,2,1,0:T(8,128)(2,1)} %coup_hbm.1, s32[1,2,128]{2,1,0:T(2,128)S(1)} %copy-done.3, s32[1]{0:T(128)S(6)} %copy.17.size_ref, ...), custom_call_target="tpu_custom_call" | custom-call | tf_op jit(solution)/shard_map/solve_and_gram/pallas_call | solution.py:466
  44.7 1.0 %copy.18 = bf16[2048,256]{1,0:T(8,128)(2,1)} copy(bf16[2048,256]{1,0:T(8,128)(2,1)S(1)} %get-tuple-element.6) | data formatting | bytes 2097152
  45.7 0.7 %copy.19 = bf16[256,256]{1,0:T(8,128)(2,1)} copy(bf16[256,256]{1,0:T(8,128)(2,1)S(1)} %get-tuple-element.7) | data formatting | bytes 262144
  46.4 0.6 %copy.20 = f32[64,256]{1,0:T(8,128)} copy(f32[64,256]{1,0:T(8,128)S(1)} %get-tuple-element.8) | data formatting | bytes 131072
Async XLA Ops:
  1.3 0.9 %copy-start = (bf16[1,256,256]{2,1,0:T(8,128)(2,1)S(1)}, bf16[1,256,256]{2,1,0:T(8,128)(2,1)}, u32[]{:S(2)}) copy-start(bf16[1,256,256]{2,1,0:T(8,128)(2,1)} %s_hbm.1) | copy-start | bytes 393220
  2.2 0.9 %copy-start.1 = (bf16[1,1,256,256]{3,2,1,0:T(8,128)(2,1)S(1)}, bf16[1,1,256,256]{3,2,1,0:T(8,128)(2,1)}, u32[]{:S(2)}) copy-start(bf16[1,1,256,256]{3,2,1,0:T(8,128)(2,1)} %u_hbm.1) | copy-start | bytes 393220
  3.1 0.9 %copy-start.2 = (bf16[256,256]{1,0:T(8,128)(2,1)S(1)}, bf16[256,256]{1,0:T(8,128)(2,1)}, u32[]{:S(2)}) copy-start(bf16[256,256]{1,0:T(8,128)(2,1)} %rhs_hbm.1) | copy-start | bytes 393220
  4.0 0.7 %copy-start.3 = (s32[1,2,128]{2,1,0:T(2,128)S(1)}, s32[1,2,128]{2,1,0:T(2,128)}, u32[]{:S(2)}) copy-start(s32[1,2,128]{2,1,0:T(2,128)} %rows_ref.1) | copy-start | bytes 3076
  4.7 0.7 %copy-start.4 = (s32[256,1]{0,1:T(1,128)S(1)}, s32[256,1]{0,1:T(1,128)}, u32[]{:S(2)}) copy-start(s32[256,1]{0,1:T(1,128)} %param.19) | copy-start | bytes 3076
  5.4 0.7 %copy-start.5 = (s32[256]{0:T(256)S(1)}, s32[256]{0:T(256)}, u32[]{:S(2)}) copy-start(s32[256]{0:T(256)} %param.20) | copy-start | bytes 3076
  6.0 0.7 %copy-start.6 = (f32[256]{0:T(256)S(1)}, f32[256]{0:T(256)}, u32[]{:S(2)}) copy-start(f32[256]{0:T(256)} %param.21) | copy-start | bytes 3076

commit v2 on v1

--- a/solution.py
+++ b/solution.py
@@ -37,15 +37,15 @@
     total_sensors,
     a_hbm,
     coup_hbm,
-    rows_ref,
+    rows_hbm,
     size_ref,
     s_hbm,
     u_hbm,
     b_hbm,
     rhs_hbm,
-    owner_ref,
-    srow_ref,
-    weight_ref,
+    owner_hbm,
+    srow_hbm,
+    weight_hbm,
     xleaf_hbm,
     xsep_ref,
     gram_ref,
@@ -70,6 +70,14 @@
     tab_in,
     wpad,
     wcol,
+    rows_ref,
+    rows_in,
+    owner_ref,
+    srow_ref,
+    weight_ref,
+    comp_v,
+    cs,
+    cr,
     gs,
     gin,
     a_sem,
@@ -77,6 +85,7 @@
     out_sem,
     anc_send,
     anc_recv,
+    fwd_send,
     tab_send,
     tab_recv,
     bf_send,
@@ -103,8 +112,34 @@
     half = pl.ds(pl.multiple_of(r * hc, hc), hc) if split else pl.ds(0, nc)
     nchunk = ls // CHUNK
 
+    barrier = pltpu.get_barrier_semaphore()
+
+    def greet(**place):
+        pl.semaphore_signal(barrier, inc=1, device_id=place, device_id_type=pl.DeviceIdType.MESH)
+
+    for j in range(n):
+        for q in range(reps):
+            @pl.when(jnp.logical_not((i == j) & (r == q)))
+            def _():
+                greet(leaf=j, rep=q)
+    for step in range(1, cols):
+        greet(col=lax.rem(c + step, cols))
+
     load_b = pltpu.make_async_copy(b_hbm, b_v, in_sem.at[0])
     load_b.start()
+    smalls = [
+        pltpu.make_async_copy(src, dst, in_sem.at[2 + k])
+        for k, (src, dst) in enumerate(
+            (
+                (rows_hbm.at[0], rows_ref),
+                (owner_hbm, owner_ref),
+                (srow_hbm, srow_ref),
+                (weight_hbm, weight_ref),
+            )
+        )
+    ]
+    for load in smalls:
+        load.start()
     load_c = pltpu.make_async_copy(coup_hbm.at[0], coup_v, in_sem.at[1])
     load_c.start()
     loads = [
@@ -115,50 +150,86 @@
     ]
     for load in loads:
         load.start()
-
-    barrier = pltpu.get_barrier_semaphore()
-
-    def greet(**place):
-        pl.semaphore_signal(barrier, inc=1, device_id=place, device_id_type=pl.DeviceIdType.MESH)
-
-    for j in range(n):
-        for q in range(reps):
-            @pl.when(jnp.logical_not((i == j) & (r == q)))
-            def _():
-                greet(leaf=j, rep=q)
-    for step in range(1, cols):
-        greet(col=lax.rem(c + step, cols))
     pl.semaphore_wait(barrier, n * reps + cols - 2)
 
-    def anc_copies(level, slot):
-        base = i // 2**level * 2**level
-        dest = base + slot
+    hs = ss // reps
+    mine = pl.ds(pl.multiple_of(r * hs, hs), hs)
+    theirs = pl.ds(pl.multiple_of((1 - r) * hs, hs), hs)
+
+    def anc_copies(level, local):
         copies = [
-            (s_hbm.at[0], s_anc.at[level - 1], 0),
+            (s_hbm.at[0, mine], s_anc.at[level - 1, mine], 0),
             (rhs_hbm.at[:, half], r_anc.at[level - 1], 1),
         ]
         if level < depth:
-            copies.append((u_hbm.at[0], u_anc.at[level - 1], 2))
-        return dest, copies
+            copies.append((u_hbm.at[0, :, mine], u_anc.at[level - 1, :, mine], 2))
+        if local:
+            copies.append((s_hbm.at[0, theirs], s_anc.at[level - 1, theirs], 3))
+            if level < depth:
+                copies.append((u_hbm.at[0, :, theirs], u_anc.at[level - 1, :, theirs], 4))
+        return copies
 
     def owner_of(level):
         return i // 2**level * 2**level + 2 ** (level - 1) - 1
 
+    def each_dest(level, act):
+        for slot in range(2**level):
+            if slot == 2 ** (level - 1) - 1:
+                continue
+
+            @pl.when(i == owner_of(level))
+            def _():
+                for src, dst, kind in anc_copies(level, False):
+                    act(
+                        remote(
+                            src,
+                            dst,
+                            anc_send.at[slot, kind],
+                            anc_recv.at[level - 1, kind],
+                            leaf=i // 2**level * 2**level + slot,
+                        )
+                    )
+
     for level in range(1, depth + 1):
-        for slot in range(2**level):
-            dest, copies = anc_copies(level, slot)
-
-            @pl.when((i == owner_of(level)) & (dest == i))
-            def _():
-                for src, dst, kind in copies:
-                    pltpu.make_async_copy(src, dst, anc_recv.at[level - 1, kind]).start()
-
-            @pl.when((i == owner_of(level)) & (dest != i))
-            def _():
-                for src, dst, kind in copies:
-                    remote(
-                        src, dst, anc_send.at[slot, kind], anc_recv.at[level - 1, kind], leaf=dest
-                    ).start()
+        each_dest(level, lambda copy: copy.start())
+
+        @pl.when(i == owner_of(level))
+        def _():
+            for src, dst, kind in anc_copies(level, True):
+                pltpu.make_async_copy(src, dst, anc_recv.at[level - 1, kind]).start()
+
+    def wait_anc(level, kinds):
+        for src, dst, kind in anc_copies(level, True):
+            if kind in kinds:
+                pltpu.make_async_copy(src, dst, anc_recv.at[level - 1, kind]).wait()
+
+    def relay_copies(level):
+        blocks = [(s_anc.at[level - 1, mine], 3)]
+        if level < depth:
+            blocks.append((u_anc.at[level - 1, :, mine], 4))
+        return [
+            remote(
+                block,
+                block,
+                fwd_send.at[level - 1, kind - 3],
+                anc_recv.at[level - 1, kind],
+                rep=1 - r,
+            )
+            for block, kind in blocks
+        ]
+
+    def relay(level):
+        wait_anc(level, (0, 2))
+
+        @pl.when(i != owner_of(level))
+        def _():
+            for copy in relay_copies(level):
+                copy.start()
+
+    for load in smalls:
+        load.wait()
+    row_copy = remote(rows_ref, rows_in, in_sem.at[6], in_sem.at[7], leaf=i ^ 1)
+    row_copy.start()
 
     hi_key = owner_ref[...] * nhi + srow_ref[...] // LANES
     lo_key = srow_ref[...] % LANES
@@ -204,8 +275,8 @@
         b_v[rows, :] = jnp.where(live(k), b_v[rows, :].astype(F32), 0.0).astype(BF16)
     load_c.wait()
     for level in range(depth):
-        hot = lax.broadcasted_iota(jnp.int32, (ss, rows_ref.shape[2]), 0) == rows_ref[
-            0, pl.ds(level, 1), :
+        hot = lax.broadcasted_iota(jnp.int32, (ss, rows_ref.shape[1]), 0) == rows_ref[
+            pl.ds(level, 1), :
         ]
         spread_v[pl.ds(level * ss, ss), :] = mm(
             hot.astype(F32).astype(BF16), coup_v[level]
@@ -216,13 +287,11 @@
         y_v[rows, :] = jnp.where(live(k), mm(a_v[rows, :], b_v[...]), 0.0).astype(BF16)
         product = mm(spread_v[:, rows], y_v[rows, half])
         part_v[...] = product if k == 0 else part_v[...] + product
-
-    def wait_anc(level, kind):
-        _, copies = anc_copies(level, 0)
-        src, dst, which = copies[kind]
-        pltpu.make_async_copy(src, dst, anc_recv.at[level - 1, which]).wait()
-
-    sent = []
+        for level in range(depth):
+            product = mm(coup_v[level, :, rows], y_v[rows, half])
+            comp_v[level] = product if k == 0 else comp_v[level] + product
+
+    sent = [row_copy]
     for level in range(1, depth + 1):
         partner = i ^ (1 << (level - 1))
         stage = level - 1
@@ -232,10 +301,13 @@
         copies = []
         for span, which in pieces:
             for m in range(span.start, span.start + span.size):
-                sbuf[stage, m] = part_v[pl.ds(m * ss, ss), :].astype(BF16)
+                if stage == 0:
+                    cs[m] = comp_v[m].astype(BF16)
+                else:
+                    sbuf[stage - 1, m] = part_v[pl.ds(m * ss, ss), :].astype(BF16)
             copy = remote(
-                sbuf.at[stage, span],
-                rbuf.at[stage, span],
+                cs.at[span] if stage == 0 else sbuf.at[stage - 1, span],
+                cr.at[span] if stage == 0 else rbuf.at[stage - 1, span],
                 bf_send.at[stage, which],
                 bf_recv.at[stage, which],
                 leaf=partner,
@@ -244,6 +316,9 @@
             copies.append(copy)
         sent += copies
         if level == 1:
+            for upper in range(1, depth + 1):
+                relay(upper)
+            row_copy.wait_recv()
             for j in range(n):
                 for q in range(reps):
                     @pl.when(jnp.logical_not((i == j) & (r == q)))
@@ -261,12 +336,18 @@
                 weights = weights + tab_in[j]
             wpad[pl.ds(0, nhi), :] = weights
             wcol[...] = wpad[...].T
-        wait_anc(level, 0)
-        wait_anc(level, 1)
-        if level < depth:
-            wait_anc(level, 2)
+
+        def received(m):
+            if level > 1:
+                return rbuf[stage - 1, m].astype(F32)
+            hot = lax.broadcasted_iota(jnp.int32, (ss, rows_in.shape[1]), 0) == rows_in[
+                pl.ds(m, 1), :
+            ]
+            return mm(hot.astype(F32).astype(BF16), cr[m])
+
+        wait_anc(level, (1, 3, 4))
         copies[0].wait_recv()
-        total = part_v[pl.ds(stage * ss, ss), :] + rbuf[stage, stage].astype(F32)
+        total = part_v[pl.ds(stage * ss, ss), :] + received(stage)
         g = (r_anc[stage].astype(F32) - total).astype(BF16)
         y_here = mm(s_anc[stage], g).astype(BF16)
         ysep[stage] = y_here
@@ -276,7 +357,7 @@
                 span = pl.ds(m * ss, ss)
                 part_v[span, :] = (
                     part_v[span, :]
-                    + rbuf[stage, m].astype(F32)
+                    + received(m)
                     + mm(u_anc[stage, m - level], y_here)
                 )
 
@@ -392,15 +473,13 @@
     for copy in sent:
         copy.wait_send()
     for level in range(1, depth + 1):
-        for slot in range(2**level):
-            dest, copies = anc_copies(level, slot)
-
-            @pl.when((i == owner_of(level)) & (dest != i))
-            def _():
-                for src, dst, kind in copies:
-                    remote(
-                        src, dst, anc_send.at[slot, kind], anc_recv.at[level - 1, kind], leaf=dest
-                    ).wait_send()
+        each_dest(level, lambda copy: copy.wait_send())
+
+        @pl.when(i != owner_of(level))
+        def _():
+            for copy in relay_copies(level):
+                copy.wait_send()
+
     for j in range(n):
         for q in range(reps):
             @pl.when(jnp.logical_not((i == j) & (r == q)))
@@ -429,6 +508,19 @@
     gram_ref[...] = gram / total_sensors
     for b in range(cols):
         scatter_gram(b, True)
+
+
+def store(x_made, sep_made, gram_made, x_out, sep_out, gram_out, sem):
+    copies = [
+        pltpu.make_async_copy(src, dst, sem.at[k])
+        for k, (src, dst) in enumerate(
+            ((x_made, x_out), (sep_made, sep_out), (gram_made, gram_out))
+        )
+    ]
+    for copy in copies:
+        copy.start()
+    for copy in copies:
+        copy.wait()
 
 
 def body(
@@ -460,18 +552,19 @@
     gram_type = BF16 if rb % 16 == 0 else F32
     nchunk = ls // CHUNK
     dma = pltpu.SemaphoreType.DMA
-    hbm = pl.BlockSpec(memory_space=pl.ANY)
+    anywhere = pl.BlockSpec(memory_space=pl.ANY)
+    hbm = pl.BlockSpec(memory_space=pltpu.HBM)
     vmem = pl.BlockSpec(memory_space=pltpu.VMEM)
     smem = pl.BlockSpec(memory_space=pltpu.SMEM)
-    return pl.pallas_call(
+    made = pl.pallas_call(
         functools.partial(kernel, n, reps, cols, sens * n * reps),
         out_shape=(
             jax.ShapeDtypeStruct((ls, nc), BF16),
             jax.ShapeDtypeStruct((ss, nc), BF16),
             jax.ShapeDtypeStruct((rb, nc), F32),
         ),
-        in_specs=[hbm, hbm, vmem, smem, hbm, hbm, hbm, hbm, vmem, vmem, vmem],
-        out_specs=(hbm, vmem, vmem),
+        in_specs=[hbm, hbm, hbm, smem, hbm, hbm, hbm, hbm, hbm, hbm, hbm],
+        out_specs=(anywhere, vmem, vmem),
         scratch_shapes=[
             pltpu.VMEM((ls, ls), BF16),
             pltpu.VMEM((ls, nc), BF16),
@@ -486,21 +579,30 @@
             pltpu.VMEM((depth, slots, ss, ss), BF16),
             pltpu.VMEM((depth, ss, hc), BF16),
             pltpu.VMEM((depth * ss, hc), F32),
-            pltpu.VMEM((depth, depth, ss, hc), BF16),
-            pltpu.VMEM((depth, depth, ss, hc), BF16),
+            pltpu.VMEM((max(depth - 1, 1), depth, ss, hc), BF16),
+            pltpu.VMEM((max(depth - 1, 1), depth, ss, hc), BF16),
             pltpu.VMEM((depth, ss, hc), BF16),
             pltpu.VMEM((depth * ss, nc), BF16),
             pltpu.VMEM((n * nhi, LANES), F32),
             pltpu.VMEM((n * reps, nhi, LANES), F32),
             pltpu.VMEM((LANES, LANES), F32),
             pltpu.VMEM((LANES, LANES), F32),
+            pltpu.VMEM((depth, kr), jnp.int32),
+            pltpu.VMEM((depth, kr), jnp.int32),
+            pltpu.VMEM((1, sens), jnp.int32),
+            pltpu.VMEM((1, sens), jnp.int32),
+            pltpu.VMEM((1, sens), F32),
+            pltpu.VMEM((depth, kr, hc), F32),
+            pltpu.VMEM((depth, kr, hc), BF16),
+            pltpu.VMEM((depth, kr, hc), BF16),
             pltpu.VMEM((cols, hc, nc), gram_type),
             pltpu.VMEM((n, rb, nc), gram_type),
             dma((nchunk,)),
-            dma((2,)),
+            dma((8,)),
             dma((nchunk,)),
             dma((n, 3)),
-            dma((depth, 3)),
+            dma((depth, 5)),
+            dma((depth, 2)),
             dma((n * reps,)),
             dma((n * reps,)),
             dma((depth, 2)),
@@ -513,7 +615,7 @@
             dma((n,)),
         ],
         compiler_params=pltpu.CompilerParams(
-            collective_id=0, has_side_effects=True, vmem_limit_bytes=52 * 2**20
+            collective_id=0, has_side_effects=True, vmem_limit_bytes=64 * 2**20 - 2**17
         ),
         name="solve_and_gram",
     )(
@@ -529,6 +631,14 @@
         sensor_row.reshape(1, sens),
         sensor_weight.reshape(1, sens),
     )
+    return pl.pallas_call(
+        store,
+        out_shape=tuple(jax.ShapeDtypeStruct(part.shape, part.dtype) for part in made),
+        in_specs=[anywhere] * 3,
+        out_specs=(hbm,) * 3,
+        scratch_shapes=[dma((3,))],
+        name="store",
+    )(*made)
 
 
 def solution(mesh):

time: 47.2 us -> 78.2 us (1.66)
  the two profiles are of different devices: /device:TPU:17 before, /device:TPU:0 now
where the time goes in v2:
time: 78.2 us; the launch traced here: 78 us
  Pallas kernels  76.7 us (98%)
  between operations  1.29 us (2%)
    pallas_call x1, Pallas kernels, body(): pl.pallas_call(store, out_shape=tuple((jax.ShapeDtypeStruct(part.shape, p...  38.9 us
    pallas_call x1, Pallas kernels, body(): pl.pallas_call(functools.partial(kernel, n, reps, cols, sens * n * reps),...  37.9 us

profile of v2, /device:TPU:0, one launch (start us, length us, event | category | flops | bytes accessed | tf_op | source)
XLA Modules:
  0.0 78.0 jit_solution(14561393789769858059)
XLA Ops:
  1.3 37.9 %solve_and_gram.1 = (bf16[2048,256]{1,0:T(8,128)(2,1)}, bf16[256,256]{1,0:T(8,128)(2,1)}, f32[64,256]{1,0:T(8,128)}) custom-call(bf16[1,2048,2048]{2,1,0:T(8,128)(2,1)} %a_hbm.1, bf16[1,2,128,2048]{3,2,1,0:T(8,128)(2,1)} %coup_hbm.1, s32[1,2,128]{2,1,0:T(2,128)} %rows_hbm.1, s32[1]{0:T(128)S(6)} %copy.14.size_ref, bf16[1,256,256]{2,1,0:T(8,128)(2,1)} %s_hbm.1, ...), custom_call_target="tpu_custom_call" | custom-call | tf_op jit(solution)/shard_map/solve_and_gram/pallas_call | solution.py:559
  39.2 38.9 %store.1 = (bf16[2048,256]{1,0:T(8,128)(2,1)}, bf16[256,256]{1,0:T(8,128)(2,1)}, f32[64,256]{1,0:T(8,128)}) custom-call(bf16[2048,256]{1,0:T(8,128)(2,1)} %get-tuple-element.6.x_made, bf16[256,256]{1,0:T(8,128)(2,1)} %get-tuple-element.7.sep_made, f32[64,256]{1,0:T(8,128)} %get-tuple-element.8.gram_made), custom_call_target="tpu_custom_call" | custom-call | tf_op jit(solution)/shard_map/store/pallas_call | solution.py:634

commit v3 on v2

--- a/solution.py
+++ b/solution.py
@@ -510,17 +510,27 @@
         scatter_gram(b, True)
 
 
-def store(x_made, sep_made, gram_made, x_out, sep_out, gram_out, sem):
-    copies = [
-        pltpu.make_async_copy(src, dst, sem.at[k])
-        for k, (src, dst) in enumerate(
-            ((x_made, x_out), (sep_made, sep_out), (gram_made, gram_out))
-        )
-    ]
-    for copy in copies:
-        copy.start()
-    for copy in copies:
-        copy.wait()
+def store(pieces, *refs):
+    made, outs, held, (load_sem, store_sem) = refs[:3], refs[3:6], refs[6:9], refs[9:]
+    moves = []
+    for k, (src, mid, dst) in enumerate(zip(made, held, outs)):
+        size = src.shape[0] // pieces[k]
+        for piece in range(pieces[k]):
+            span = pl.ds(piece * size, size)
+            sem = len(moves)
+            moves.append(
+                (
+                    pltpu.make_async_copy(src.at[span], mid.at[span], load_sem.at[sem]),
+                    pltpu.make_async_copy(mid.at[span], dst.at[span], store_sem.at[sem]),
+                )
+            )
+    for load, _ in moves:
+        load.start()
+    for load, save in moves:
+        load.wait()
+        save.start()
+    for _, save in moves:
+        save.wait()
 
 
 def body(
@@ -631,12 +641,15 @@
         sensor_row.reshape(1, sens),
         sensor_weight.reshape(1, sens),
     )
+    pieces = (nchunk, 1, 1)
     return pl.pallas_call(
-        store,
+        functools.partial(store, pieces),
         out_shape=tuple(jax.ShapeDtypeStruct(part.shape, part.dtype) for part in made),
         in_specs=[anywhere] * 3,
-        out_specs=(hbm,) * 3,
-        scratch_shapes=[dma((3,))],
+        out_specs=(anywhere,) * 3,
+        scratch_shapes=[pltpu.VMEM(part.shape, part.dtype) for part in made]
+        + [dma((sum(pieces),)), dma((sum(pieces),))],
+        compiler_params=pltpu.CompilerParams(vmem_limit_bytes=64 * 2**20 - 2**17),
         name="store",
     )(*made)
 

time: 78.2 us -> 41.5 us (0.53)
  Pallas kernels: 76.7 us -> 40.1 us
    pallas_call x1, Pallas kernels: 38.9 us -> 2.18 us  [body(): pl.pallas_call(functools.partial(store, pieces), out_shape=tuple((jax.Sha...]
where the time goes in v3:
time: 41.5 us; the launch traced here: 41.4 us
  Pallas kernels  40.1 us (97%)
  between operations  1.29 us (3%)
    pallas_call x1, Pallas kernels, body(): pl.pallas_call(functools.partial(kernel, n, reps, cols, sens * n * reps),...  37.9 us
    pallas_call x1, Pallas kernels, body(): pl.pallas_call(functools.partial(store, pieces), out_shape=tuple((jax.Sha...  2.18 us

profile of v3, /device:TPU:0, one launch (start us, length us, event | category | flops | bytes accessed | tf_op | source)
XLA Modules:
  0.0 41.4 jit_solution(10452419308525700702)
XLA Ops:
  1.3 37.9 %solve_and_gram.1 = (bf16[2048,256]{1,0:T(8,128)(2,1)}, bf16[256,256]{1,0:T(8,128)(2,1)}, f32[64,256]{1,0:T(8,128)}) custom-call(bf16[1,2048,2048]{2,1,0:T(8,128)(2,1)} %a_hbm.1, bf16[1,2,128,2048]{3,2,1,0:T(8,128)(2,1)} %coup_hbm.1, s32[1,2,128]{2,1,0:T(2,128)} %rows_hbm.1, s32[1]{0:T(128)S(6)} %copy.14.size_ref, bf16[1,256,256]{2,1,0:T(8,128)(2,1)} %s_hbm.1, ...), custom_call_target="tpu_custom_call" | custom-call | tf_op jit(solution)/shard_map/solve_and_gram/pallas_call | solution.py:569
  39.2 2.2 %store.1 = (bf16[2048,256]{1,0:T(8,128)(2,1)}, bf16[256,256]{1,0:T(8,128)(2,1)}, f32[64,256]{1,0:T(8,128)}) custom-call(bf16[2048,256]{1,0:T(8,128)(2,1)} %get-tuple-element.6.refs_0_, bf16[256,256]{1,0:T(8,128)(2,1)} %get-tuple-element.7.refs_1_, f32[64,256]{1,0:T(8,128)} %get-tuple-element.8.refs_2_), custom_call_target="tpu_custom_call" | custom-call | tf_op jit(solution)/shard_map/store/pallas_call | solution.py:645
